TPU v7x, 1024 devices: a whole 4x4x32 slice. The times are simulated.
1024 devices in a mesh: dp: 32 (over z_hi, x, core), tensor: 32 (over y, z_lo).
Axes of the slice: x: 4, y: 4, z: 32 (z_hi: 4, z_lo: 8; z = z_hi * 8 + z_lo), core: 2. Of those that a mesh axis runs over, the one named last changes fastest.
Arguments:
- hidden: bfloat16 [6144, 14336], P('dp', 'tensor'), parts along dimension 0, may hold values from -6 to 6
- down_weight: bfloat16 [14336, 8192], P('tensor'), may hold values from -0.046875 to 0.046875
- residual: bfloat16 [6144, 8192], P('dp', 'tensor'), parts along dimension 0, may hold values from -100 to 100
- norm_gain: float32 [8192], replicated, may hold values from 0.1 to 1.9
- qkv_weight: bfloat16 [8192, 5120], P(None, 'tensor'), may hold values from -0.0625 to 0.0625
Outputs:
- stream: bfloat16 [6144, 8192], P('dp', 'tensor'), parts along dimension 0
- qkv: bfloat16 [6144, 5120], P('dp', 'tensor'), parts along dimension 0
There are 32 independent parts, one for each index of `dp`. A program takes and returns all parts, laid end to end along the dimension named above; an argument that names none is the same for every part. Nothing has to cross between parts.
All inputs are finite; a program needn't handle non-finite values.
Results may differ from a plain program's by a relative error of at most 0.02.
Values may be sent and summed in bfloat16 or wider, within the bound.
A program may use at most 64 MiB of HBM per device.

v0:
```python
import jax
import jax.numpy as jnp
from jax import lax
from jax.sharding import PartitionSpec as P

epsilon = 1e-05


def shards(hidden, down_weight, residual, norm_gain, qkv_weight):
    partial_sum = lax.psum_scatter(
        jnp.dot(hidden, down_weight, preferred_element_type=jnp.float32).astype(jnp.bfloat16),
        "tensor",
        scatter_dimension=0,
        tiled=True,
    ).astype(jnp.float32)
    res_rows = lax.all_to_all(residual, "tensor", split_axis=0, concat_axis=1, tiled=True)
    summed = partial_sum + res_rows.astype(jnp.float32)
    scale = jnp.sqrt(jnp.mean(summed * summed, axis=1, keepdims=True) + epsilon)
    normed = (summed / scale * norm_gain[None, :]).astype(jnp.bfloat16)
    stream = lax.all_to_all(
        summed.astype(jnp.bfloat16), "tensor", split_axis=1, concat_axis=0, tiled=True
    )
    qkv = jnp.dot(
        lax.all_gather(normed, "tensor", axis=0, tiled=True),
        qkv_weight,
        preferred_element_type=jnp.float32,
    ).astype(jnp.bfloat16)
    return (stream, qkv)


def solution(mesh):
    in_specs = (P("dp", "tensor"), P("tensor", None), P("dp", "tensor"), P(), P(None, "tensor"))
    out_specs = (P("dp", "tensor"), P("dp", "tensor"))
    return jax.shard_map(shards, mesh=mesh, in_specs=in_specs, out_specs=out_specs, check_vma=False)
```

profile of v0, /device:TPU:38, one launch (start us, length us, event | category | flops | bytes accessed | tf_op | source)
XLA Modules:
  0.0 508.3 jit_solution(6529850336566540748)
XLA Ops:
  7.2 0.0 copy-start
  7.2 1.7 all_to_all.24
  8.9 15.4 %all-to-all-start = ((bf16[32,6,256]{2,1,0:T(8,128)(2,1)}), bf16[32,6,256]{2,1,0:T(8,128)(2,1)S(1)}, u32[]{:S(2)}, u32[]{:S(2)}) async-start(bf16[32,6,256]{2,1,0:T(8,128)(2,1)} %all_to_all.24), calls=%async_computation | async-start | bytes 262144 | tf_op jit(solution)/shard_map/all_to_all | solution.py:16
  24.3 0.0 all-gather.3.cloned.1.call-start
  24.4 6.6 %convolution_convert_fusion = bf16[192,8192]{1,0:T(8,128)(2,1)} fusion(bf16[192,448]{1,0:T(8,128)(2,1)} %param.5, bf16[448,8192]{1,0:T(8,128)(2,1)} %param.6), kind=kOutput, calls=%fused_computation | convolution fusion | flops 1410859008 | bytes 10657792 | tf_op jit(solution)/shard_map/dot_general | solution.py:11
  31.0 145.4 %fusion = bf16[8,8192]{1,0:T(8,128)(2,1)S(1)} fusion(bf16[192,8192]{1,0:T(8,128)(2,1)} %convolution_convert_fusion), kind=kCustom, calls=%all-reduce-scatter | all-reduce-scatter fusion | flops 2097153 | bytes 3280896
  176.5 1.3 collective-permute-start.6
  177.8 1.3 collective-permute-start.5
  179.1 2.7 collective-permute-start.7
  181.8 1.3 collective-permute-start.4
  183.1 15.4 %collective-permute-start.3 = (bf16[8,8192]{1,0:T(8,128)(2,1)S(1)}, bf16[8,8192]{1,0:T(8,128)(2,1)S(1)}, u32[]{:S(2)}, u32[]{:S(2)}) collective-permute-start(bf16[8,8192]{1,0:T(8,128)(2,1)S(1)} %fusion), channel_id=1, source_target_pairs={{0,4},{1,5},{2,6},{3,7},{4,8},{5,9},{6,10},{7,11},{8,12},{9,13},{1... | collective-permute-start | bytes 393224
  198.5 0.0 collective-permute-done.7
  198.6 1.9 collective-permute-start.2
  200.5 0.0 collective-permute-done.6
  200.5 4.0 collective-permute-start.1
  204.5 0.0 collective-permute-done.5
  204.5 2.7 collective-permute-start
  207.3 1.3 dynamic-slice.4
  209.2 0.0 collective-permute-done.4
  209.2 0.0 collective-permute-done.3
  209.2 0.0 collective-permute-done.2
  209.2 0.0 collective-permute-done.1
  209.2 2.2 collective-permute-done
  211.5 25.3 %concatenate = bf16[70,8192]{1,0:T(8,128)(2,1)} concatenate(bf16[6,8192]{1,0:T(8,128)(2,1)S(1)} %collective-permute-done.7, bf16[8,8192]{1,0:T(8,128)(2,1)S(1)} %collective-permute-done.6, bf16[8,8192]{1,0:T(8,128)(2,1)S(1)} %collective-permute-done.5, bf16[8,8192]{1,0:T(8,128)(2,1)S(1)} %collective-permute-done.4, bf16[8,8192]{1,0:T(8,128)(2,1)S(1)} %collective-permute-done.3, ...), dimensions={0} | concatenate | bytes 2293760
  236.7 0.0 all-to-all-done
  236.8 1.1 multiply_reduce_fusion
  237.9 1.7 fusion.1
  239.6 0.0 all-gather.3.cloned.1.call-update
  239.7 25.0 %all_to_all.32 = bf16[6,32,256]{2,0,1:T(8,128)(2,1)S(1)} all-to-all(bf16[6,32,256]{2,0,1:T(8,128)(2,1)S(1)} %bitcast.17), channel_id=1, replica_groups=mesh['dp'=32,'tensor'=32] {'tensor'}, dimensions={1} | all-to-all | bytes 196608 | tf_op jit(solution)/shard_map/all_to_all | solution.py:20
  264.7 0.7 all_to_all.29
  265.4 227.4 %all-gather.3.cloned.1.call-done = bf16[32,6,8192]{2,1,0:T(8,128)(2,1)} async-done(((bf16[1,6,8192]{2,1,0:T(8,128)(2,1)}), bf16[32,6,8192]{2,1,0:T(8,128)(2,1)}) %all-gather.3.cloned.1.call-update) | async-done | bytes 3145744 | tf_op jit(solution)/shard_map/all_gather | solution.py:24
  492.8 4.9 reshape.23
  497.7 0.0 copy-done
  497.7 3.7 convolution_convert_fusion.1
  (3 shorter events, 0.1 us)
Async XLA Ops:
  7.2 490.5 %copy-start = (bf16[8192,160]{0,1:T(8,128)(2,1)S(1)}, bf16[8192,160]{0,1:T(8,128)(2,1)}, u32[]{:S(2)}) copy-start(bf16[8192,160]{0,1:T(8,128)(2,1)} %param.9) | copy-start | bytes 7864324
  8.9 227.8 %all-to-all-start = ((bf16[32,6,256]{2,1,0:T(8,128)(2,1)}), bf16[32,6,256]{2,1,0:T(8,128)(2,1)S(1)}, u32[]{:S(2)}, u32[]{:S(2)}) async-start(bf16[32,6,256]{2,1,0:T(8,128)(2,1)} %all_to_all.24), calls=%async_computation | async-start | bytes 262144 | tf_op jit(solution)/shard_map/all_to_all | solution.py:16
  24.3 468.4 %all-gather.3.cloned.1.call-start = ((), (), s32[]{:S(2)}) async-start(), calls=%async_computation.2 | async-start | bytes 4325376 | tf_op jit(solution)/shard_map/all_gather | solution.py:24
  176.5 24.0 %collective-permute-start.6 = (bf16[8,8192]{1,0:T(8,128)(2,1)S(1)}, bf16[8,8192]{1,0:T(8,128)(2,1)S(1)}, u32[]{:S(2)}, u32[]{:S(2)}) collective-permute-start(bf16[8,8192]{1,0:T(8,128)(2,1)S(1)} %fusion), channel_id=1, source_target_pairs={{0,7},{1,8},{2,9},{3,10},{4,11},{5,12},{6,13},{7,14},{8,15},{9,16}... | collective-permute-start | bytes 393224
  177.8 26.7 %collective-permute-start.5 = (bf16[8,8192]{1,0:T(8,128)(2,1)S(1)}, bf16[8,8192]{1,0:T(8,128)(2,1)S(1)}, u32[]{:S(2)}, u32[]{:S(2)}) collective-permute-start(bf16[8,8192]{1,0:T(8,128)(2,1)S(1)} %fusion), channel_id=1, source_target_pairs={{0,6},{1,7},{2,8},{3,9},{4,10},{5,11},{6,12},{7,13},{8,14},{9,15},... | collective-permute-start | bytes 393224
  179.1 19.4 %collective-permute-start.7 = (bf16[6,8192]{1,0:T(8,128)(2,1)S(1)}, bf16[6,8192]{1,0:T(8,128)(2,1)S(1)}, u32[]{:S(2)}, u32[]{:S(2)}) collective-permute-start(bf16[6,8192]{1,0:T(8,128)(2,1)S(1)} %slice), channel_id=1, source_target_pairs={{0,8},{1,9},{2,10},{3,11},{4,12},{5,13},{6,14},{7,15},{8,16},{9,17... | collective-permute-start | bytes 294920
  181.8 27.4 %collective-permute-start.4 = (bf16[8,8192]{1,0:T(8,128)(2,1)S(1)}, bf16[8,8192]{1,0:T(8,128)(2,1)S(1)}, u32[]{:S(2)}, u32[]{:S(2)}) collective-permute-start(bf16[8,8192]{1,0:T(8,128)(2,1)S(1)} %fusion), channel_id=1, source_target_pairs={{0,5},{1,6},{2,7},{3,8},{4,9},{5,10},{6,11},{7,12},{8,13},{9,14},{... | collective-permute-start | bytes 393224
  183.1 26.1 %collective-permute-start.3 = (bf16[8,8192]{1,0:T(8,128)(2,1)S(1)}, bf16[8,8192]{1,0:T(8,128)(2,1)S(1)}, u32[]{:S(2)}, u32[]{:S(2)}) collective-permute-start(bf16[8,8192]{1,0:T(8,128)(2,1)S(1)} %fusion), channel_id=1, source_target_pairs={{0,4},{1,5},{2,6},{3,7},{4,8},{5,9},{6,10},{7,11},{8,12},{9,13},{1... | collective-permute-start | bytes 393224
  198.6 10.7 %collective-permute-start.2 = (bf16[8,8192]{1,0:T(8,128)(2,1)S(1)}, bf16[8,8192]{1,0:T(8,128)(2,1)}, u32[]{:S(2)}, u32[]{:S(2)}) collective-permute-start(bf16[8,8192]{1,0:T(8,128)(2,1)S(1)} %fusion), channel_id=1, source_target_pairs={{0,3},{1,4},{2,5},{3,6},{4,7},{5,8},{6,9},{7,10},{8,11},{9,12},{10... | collective-permute-start | bytes 393224
  200.5 8.7 %collective-permute-start.1 = (bf16[8,8192]{1,0:T(8,128)(2,1)S(1)}, bf16[8,8192]{1,0:T(8,128)(2,1)}, u32[]{:S(2)}, u32[]{:S(2)}) collective-permute-start(bf16[8,8192]{1,0:T(8,128)(2,1)S(1)} %fusion), channel_id=1, source_target_pairs={{0,2},{1,3},{2,4},{3,5},{4,6},{5,7},{6,8},{7,9},{8,10},{9,11},{10,... | collective-permute-start | bytes 393224
  204.5 7.0 %collective-permute-start = (bf16[8,8192]{1,0:T(8,128)(2,1)S(1)}, bf16[8,8192]{1,0:T(8,128)(2,1)}, u32[]{:S(2)}, u32[]{:S(2)}) collective-permute-start(bf16[8,8192]{1,0:T(8,128)(2,1)S(1)} %fusion), channel_id=1, source_target_pairs={{0,1},{1,2},{2,3},{3,4},{4,5},{5,6},{6,7},{7,8},{8,9},{9,10},{10,1... | collective-permute-start | bytes 393224
Sparse Core Ops, SparseCore 0:
  239.8 252.9 all-gather.2
where the time goes:
time: 510 us; the launch traced here: 508 us
  waiting for transfers between devices  230 us (45%)
  blocking collectives  170 us (33%)
  starting transfers between devices  46.1 us (9%)
  local copies, waits for them, and re-layouts  33.9 us (7%)
  between operations  14.8 us (3%)
  matrix products  10.4 us (2%)
    all_gather x1, waiting for transfers between devices, shards(): lax.all_gather(normed, 'tensor', axis=0, tiled=True)  227 us
    unnamed x1, blocking collectives  145 us
    unnamed x6, local copies, waits for them, and re-layouts  31.5 us
    unnamed x8, starting transfers between devices  30.7 us
    all_to_all x1, blocking collectives, shards(): lax.all_to_all(summed.astype(jnp.bfloat16), 'tensor', split_axis=1, conca...  25 us
    all_to_all x1, starting transfers between devices, shards(): lax.all_to_all(residual, 'tensor', split_axis=0, concat_axis=1, tiled=True)  15.4 us
  transfers between devices with their start and end apart: 10, of which 2 were waited for; matrix products, arithmetic and copies ran while one was open for 35% of the time, Pallas kernels for 0%

commit v1 on v0

v1 whole, which is shorter than its diff:
```python
import jax
import jax.numpy as jnp
from jax import lax
from jax.experimental import pallas as pl
from jax.experimental.pallas import tpu as pltpu
from jax.sharding import PartitionSpec as P

EPS = 1e-05
T = 192
W = 256
NQ = 160
D = 8192
FG = 448
CHUNKS = ((0, 64), (64, 64), (128, 64))
NC = len(CHUNKS)
F32 = jnp.float32
BF16 = jnp.bfloat16
MESH = pl.DeviceIdType.MESH


def times_t(a, b):
    return lax.dot_general(a, b, (((1,), (1,)), ((), ())), preferred_element_type=F32)


def kernel(
    hid_hbm, wd_hbm, res_hbm, gain_hbm, wq_hbm,
    stream_ref, qkv_ref,
    hid, wd, res, gain, wq,
    wq0, part, y2a, y2b, y3l, y3r,
    s, zr, agg, aggs, zx, sg, acc, fs, fr,
    lsem, wsem,
    y1s, y1r, y2s, y2r, y3s, y3r_sem,
    z1s, z1r, z2s, z2r, gs, gr, fss, frs,
    q1s, q1r, q2s, q2r,
):
    t = lax.axis_index("tensor")
    dp = lax.axis_index("dp")
    y = t // 8
    z = t % 8
    h = z // 4
    l = z % 4
    rep = dp % 8
    dpb = dp - rep

    def at_y(k):
        return {"tensor": ((y + k) % 4) * 8 + z}

    def quad_l(m):
        lo = l % 2
        hi = l // 2
        if m % 2:
            lo = 1 - lo
        if m // 2:
            hi = 1 - hi
        return hi * 2 + lo

    def at_quad(m):
        return {"tensor": y * 8 + h * 4 + quad_l(m)}

    at_half = {"tensor": y * 8 + (1 - h) * 4 + l}

    def at_rep(m):
        return {"dp": dpb + (rep + m) % 8}

    right, left, across = at_y(1), at_y(3), at_y(2)
    peers = [right, left, across, at_half]
    peers += [at_quad(m) for m in (1, 2, 3)]
    peers += [at_rep(m) for m in range(1, 8)]

    def wd_copy(k):
        col = pl.multiple_of(((y + k) % 4) * 2048, 2048)
        return pltpu.make_async_copy(wd_hbm.at[:, pl.ds(col, 2048)], wd.at[k], wsem.at[k])

    c_hid = pltpu.make_async_copy(hid_hbm, hid, lsem.at[0])
    c_res = pltpu.make_async_copy(res_hbm, res, lsem.at[1])
    c_gain = pltpu.make_async_copy(gain_hbm, gain, lsem.at[2])
    own = pl.multiple_of(y * 2048, 2048)
    c_wq = pltpu.make_async_copy(wq_hbm.at[:, pl.ds(own, 2048)], wq0, lsem.at[3])
    c_hid.start()
    wd_copy(2).start()

    barrier = pltpu.get_barrier_semaphore()
    for p in peers:
        pl.semaphore_signal(barrier, 1, device_id=p, device_id_type=MESH)

    wd_copy(1).start()
    wd_copy(3).start()
    wd_copy(0).start()
    c_wq.start()
    c_res.start()
    c_gain.start()

    def remote(src, dst, ss, rs, dev):
        return pltpu.make_async_remote_copy(
            src_ref=src, dst_ref=dst, send_sem=ss, recv_sem=rs, device_id=dev, device_id_type=MESH
        )

    def matmul(k):
        wd_copy(k).wait()

        def body(j, c):
            cols = pl.ds(pl.multiple_of(j * W, W), W)
            part[k, j] = jnp.dot(hid[...], wd[k, :, cols], preferred_element_type=F32).astype(BF16)
            return c

        lax.fori_loop(0, 8, body, 0)

    def tok(c):
        return pl.ds(CHUNKS[c][0], CHUNKS[c][1])

    LO, HI = pl.ds(0, 4), pl.ds(4, 4)

    def wq_cols(owner):
        return pl.ds(pl.multiple_of(owner * 2048 + rep * W, W), W)

    def q1(k):
        src = wq_hbm.at[:, wq_cols((y + k) % 4)]
        return remote(src, wq.at[rep, 3 - k], q1s.at[k - 1], q1r.at[3 - k], at_y(k))

    def q1_recv(k):
        src = wq_hbm.at[:, wq_cols(y)]
        return remote(src, wq.at[rep, k - 1], q1s.at[3 - k], q1r.at[k - 1], at_y(k))

    def q2(m):
        blk = wq.at[rep]
        return remote(blk, blk, q2s.at[m - 1], q2r.at[m - 1], at_rep(m))

    def q2_recv(m):
        blk = wq.at[(rep + 8 - m) % 8]
        return remote(blk, blk, q2s.at[m - 1], q2r.at[m - 1], at_rep(m))

    def y1(c):
        return (
            remote(part.at[2, LO, tok(c)], y2a.at[:, tok(c)], y1s.at[0, c], y1r.at[0, c], right),
            remote(part.at[2, HI, tok(c)], y2b.at[:, tok(c)], y1s.at[1, c], y1r.at[1, c], left),
        )

    def y2(c):
        return (
            remote(part.at[1, HI, tok(c)], y3l.at[HI, tok(c)], y2s.at[0, c], y2r.at[0, c], right),
            remote(part.at[3, LO, tok(c)], y3r.at[LO, tok(c)], y2s.at[1, c], y2r.at[1, c], left),
        )

    def y3(c):
        return (
            remote(y2a.at[:, tok(c)], y3l.at[LO, tok(c)], y3s.at[0, c], y3r_sem.at[0, c], right),
            remote(y2b.at[:, tok(c)], y3r.at[HI, tok(c)], y3s.at[1, c], y3r_sem.at[1, c], left),
        )

    def start(ds):
        for d in ds:
            d.start()

    def aug(c):
        ra, rb = y1(c)
        ra.wait_recv()

        def body_a(j, x):
            y2a[j, tok(c)] = (y2a[j, tok(c)].astype(F32) + part[1, j, tok(c)].astype(F32)).astype(BF16)
            return x

        lax.fori_loop(0, 4, body_a, 0)
        y3(c)[0].start()
        rb.wait_recv()

        def body_b(j, x):
            y2b[j, tok(c)] = (y2b[j, tok(c)].astype(F32) + part[3, 4 + j, tok(c)].astype(F32)).astype(BF16)
            return x

        lax.fori_loop(0, 4, body_b, 0)
        y3(c)[1].start()

    def z1(c, m):
        dst = quad_l(m)
        return remote(s.at[:, dst, tok(c)], zr.at[m - 1, :, tok(c)], z1s.at[m - 1, c], z1r.at[m - 1, c], at_quad(m))

    def ysum(c):
        for d in y2(c) + y3(c):
            d.wait_recv()

        def body(j, x):
            v = part[0, j, tok(c)].astype(F32) + y3l[j, tok(c)].astype(F32) + y3r[j, tok(c)].astype(F32)
            s[j // 4, j % 4, tok(c)] = v.astype(BF16)
            return x

        lax.fori_loop(0, 8, body, 0)
        for m in (3, 2, 1):
            z1(c, m).start()

    def z2(c):
        return remote(aggs.at[:, tok(c)], zx.at[:, tok(c)], z2s.at[c], z2r.at[c], at_half)

    def zsum(c):
        for m in (1, 2, 3):
            z1(c, m).wait_recv()

        def body(hh, x):
            v = s[hh, l, tok(c)].astype(F32) + zr[0, hh, tok(c)].astype(F32)
            v = v + zr[1, hh, tok(c)].astype(F32) + zr[2, hh, tok(c)].astype(F32)
            mine = jnp.where(hh == h, 1.0, 0.0).astype(F32)
            v = v + res[tok(c)].astype(F32) * mine
            agg[hh, tok(c)] = v
            aggs[hh, tok(c)] = v.astype(BF16)
            return x

        lax.fori_loop(0, 2, body, 0)
        z2(c).start()

    def g(c, m):
        blk = sg.at[:, l, tok(c)]
        return remote(blk, blk, gs.at[m - 1, c], gr.at[m - 1, c], at_quad(m))

    def g_recv(c, m):
        blk = sg.at[:, quad_l(m), tok(c)]
        return remote(blk, blk, gs.at[m - 1, c], gr.at[m - 1, c], at_quad(m))

    def gather(c):
        z2(c).wait_recv()

        def body(hh, x):
            v = agg[hh, tok(c)] + zx[hh, tok(c)].astype(F32)
            sg[hh, l, tok(c)] = v.astype(BF16)
            return x

        lax.fori_loop(0, 2, body, 0)
        for m in (3, 2, 1):
            g(c, m).start()
        stream_ref[tok(c)] = sg[h, l, tok(c)]

    def f(c, k):
        return remote(fs.at[k - 1, tok(c)], fr.at[3 - k, tok(c)], fss.at[k - 1, c], frs.at[3 - k, c], at_y(k))

    def f_recv(c, k):
        return remote(fs.at[3 - k, tok(c)], fr.at[k - 1, tok(c)], fss.at[3 - k, c], frs.at[k - 1, c], at_y(k))

    def project(c):
        n = CHUNKS[c][1]
        for m in (1, 2, 3):
            g_recv(c, m).wait_recv()
        acc[:, tok(c)] = jnp.zeros((4, n, W), F32)

        def body(j, sq):
            v = sg[j // 4, j % 4, tok(c)].astype(F32)
            cols = pl.ds(pl.multiple_of(y * 2048 + j * W, W), W)
            x = (v * gain[:, cols]).astype(BF16)
            mine = pl.ds(pl.multiple_of(j * W, W), W)
            acc[0, tok(c), pl.ds(0, NQ)] += times_t(x, wq0[:, mine])
            for k in (1, 2, 3):
                acc[k, tok(c), pl.ds(0, NQ)] += times_t(x, wq[j, k - 1])
            return sq + jnp.sum(v * v, axis=1, keepdims=True)

        sq = lax.fori_loop(0, 8, body, jnp.zeros((n, 1), F32))
        lane = lax.broadcasted_iota(jnp.int32, (n, W), 1)
        hi = sq.astype(BF16).astype(F32)
        for k in (2, 1, 3):
            v = jnp.where(lane < NQ, acc[k, tok(c)], jnp.where(lane == NQ, hi, sq - hi))
            fs[k - 1, tok(c)] = v.astype(BF16)
            f(c, k).start()
        acc[0, tok(c)] = jnp.where(lane < NQ, acc[0, tok(c)], jnp.where(lane == NQ, hi, sq - hi))

    def finish(c):
        n = CHUNKS[c][1]
        v = acc[0, tok(c)]
        for k in (1, 3, 2):
            f_recv(c, k).wait_recv()
            v = v + fr[k - 1, tok(c)].astype(F32)
        lane = lax.broadcasted_iota(jnp.int32, (n, W), 1)
        extra = jnp.where((lane == NQ) | (lane == NQ + 1), v, 0.0)
        sq = jnp.sum(extra, axis=1, keepdims=True)
        v = v / jnp.sqrt(sq * (1.0 / D) + EPS)
        qkv_ref[tok(c)] = v[:, :NQ].astype(BF16)

    c_hid.wait()
    matmul(2)
    pl.semaphore_wait(barrier, len(peers))
    start(y1(0))
    for k in (2, 1, 3):
        q1(k).start()
    matmul(1)
    y2(0)[0].start()
    matmul(3)
    y2(0)[1].start()
    if NC > 1:
        start(y1(1))
    matmul(0)
    c_wq.wait()
    c_res.wait()
    c_gain.wait()

    def y_step(c):
        aug(c)
        if c == 0:
            for k in (1, 2, 3):
                q1_recv(k).wait_recv()
            for m in (4, 2, 3, 5, 6, 7, 1):
                q2(m).start()
        if c + 1 < NC:
            start(y2(c + 1))
        if c + 2 < NC:
            start(y1(c + 2))
        ysum(c)

    def run(stage, c):
        if stage == 0:
            y_step(c)
        elif stage == 1:
            zsum(c)
        elif stage == 2:
            gather(c)
        elif stage == 3:
            if c == 0:
                for m in range(1, 8):
                    q2_recv(m).wait_recv()
            project(c)
        else:
            finish(c)

    offsets = (0.0, 9.0, 16.0, 25.0, 30.0)
    period = 24.0 / NC
    order = sorted((c * period + offsets[st], st, c) for c in range(NC) for st in range(5))
    for _, st, c in order:
        run(st, c)

    for k in (1, 2, 3):
        q1(k).wait_send()
    for m in range(1, 8):
        q2(m).wait_send()
    for c in range(NC):
        for d in y1(c) + y2(c) + y3(c):
            d.wait_send()
        for m in (1, 2, 3):
            z1(c, m).wait_send()
            g(c, m).wait_send()
            f(c, m).wait_send()
        z2(c).wait_send()


def shards(hidden, down_weight, residual, norm_gain, qkv_weight):
    hbm = pl.BlockSpec(memory_space=pltpu.MemorySpace.HBM)
    vmem = pl.BlockSpec(memory_space=pltpu.VMEM)
    dma = pltpu.SemaphoreType.DMA
    return pl.pallas_call(
        kernel,
        out_shape=(jax.ShapeDtypeStruct((T, W), BF16), jax.ShapeDtypeStruct((T, NQ), BF16)),
        in_specs=[hbm] * 5,
        out_specs=(vmem, vmem),
        scratch_shapes=[
            pltpu.VMEM((T, FG), BF16),
            pltpu.VMEM((4, FG, 2048), BF16),
            pltpu.VMEM((T, W), BF16),
            pltpu.VMEM((1, D), F32),
            pltpu.VMEM((8, 3, NQ, W), BF16),
            pltpu.VMEM((NQ, 2048), BF16),
            pltpu.VMEM((4, 8, T, W), BF16),
            pltpu.VMEM((4, T, W), BF16),
            pltpu.VMEM((4, T, W), BF16),
            pltpu.VMEM((8, T, W), BF16),
            pltpu.VMEM((8, T, W), BF16),
            pltpu.VMEM((2, 4, T, W), BF16),
            pltpu.VMEM((3, 2, T, W), BF16),
            pltpu.VMEM((2, T, W), F32),
            pltpu.VMEM((2, T, W), BF16),
            pltpu.VMEM((2, T, W), BF16),
            pltpu.VMEM((2, 4, T, W), BF16),
            pltpu.VMEM((4, T, W), F32),
            pltpu.VMEM((3, T, W), BF16),
            pltpu.VMEM((3, T, W), BF16),
            dma((4,)), dma((4,)),
            dma((2, NC)), dma((2, NC)), dma((2, NC)), dma((2, NC)), dma((2, NC)), dma((2, NC)),
            dma((3, NC)), dma((3, NC)), dma((NC,)), dma((NC,)),
            dma((3, NC)), dma((3, NC)), dma((3, NC)), dma((3, NC)),
            dma((3,)), dma((3,)), dma((7,)), dma((7,)),
        ],
        compiler_params=pltpu.CompilerParams(
            collective_id=0, has_side_effects=True, vmem_limit_bytes=60 * 1024 * 1024
        ),
        cost_estimate=pl.CostEstimate(flops=1_900_000_000, bytes_accessed=12_000_000, transcendentals=0),
        name="down_norm_qkv",
    )(
        hidden,
        down_weight,
        residual,
        norm_gain.reshape(1, D),
        qkv_weight.T,
    )


def solution(mesh):
    in_specs = (P("dp", "tensor"), P("tensor", None), P("dp", "tensor"), P(), P(None, "tensor"))
    out_specs = (P("dp", "tensor"), P("dp", "tensor"))
    return jax.shard_map(shards, mesh=mesh, in_specs=in_specs, out_specs=out_specs, check_vma=False)
```

time: 510 us -> 94.1 us (0.18)
  the two profiles are of different devices: /device:TPU:38 before, /device:TPU:256 now
where the time goes in v1:
time: 94.1 us; the launch traced here: 93.9 us
  Pallas kernels  90 us (96%)
  local copies, waits for them, and re-layouts  3.17 us (3%)
    pallas_call x1, Pallas kernels, shards(): pl.pallas_call(kernel, out_shape=(jax.ShapeDtypeStruct((T, W), BF16), jax...  90 us

profile of v1, /device:TPU:256, one launch (start us, length us, event | category | flops | bytes accessed | tf_op | source)
XLA Modules:
  0.0 93.9 jit_solution(13168015988540887040)
XLA Ops:
  0.6 90.0 %down_norm_qkv.1 = (bf16[192,256]{1,0:T(8,128)(2,1)}, bf16[192,160]{1,0:T(8,128)(2,1)}) custom-call(bf16[192,448]{1,0:T(8,128)(2,1)} %hid_hbm.1, bf16[448,8192]{1,0:T(8,128)(2,1)} %wd_hbm.1, bf16[192,256]{1,0:T(8,128)(2,1)} %res_hbm.1, f32[1,8192]{1,0:T(1,128)} %bitcast.3, bf16[160,8192]{1,0:T(8,128)(2,1)} %bitcast.2), custom_call_target="tpu_custom_call" | custom-call | flops 1900000000 | bytes 12000000 | tf_op jit(solution)/shard_map/down_norm_qkv/pallas_call | solution.py:342
  90.7 1.6 %copy.7 = bf16[192,160]{0,1:T(8,128)(2,1)} copy(bf16[192,160]{1,0:T(8,128)(2,1)} %get-tuple-element.3) | data formatting | bytes 122880 | tf_op jit(solution)/shard_map/down_norm_qkv/pallas_call | solution.py:342
  92.3 1.5 %copy.9 = bf16[192,256]{1,0:T(8,128)(2,1)} copy(bf16[192,256]{1,0:T(8,128)(2,1)} %get-tuple-element.6) | data formatting | bytes 196608

commit v2 on v1

--- a/solution.py
+++ b/solution.py
@@ -11,8 +11,17 @@
 NQ = 160
 D = 8192
 FG = 448
-CHUNKS = ((0, 64), (64, 64), (128, 64))
+CHUNKS = ((0, 48), (48, 48), (96, 48), (144, 48))
 NC = len(CHUNKS)
+GATE_Z = (0, 0, 0, 0)
+GATE_G = (1, 0, 0, 0)
+ORDER = (
+    "A0", "M1", "M3", "B0", "Q1", "Q3", "M0", "A1", "a0", "B1",
+    "A2", "Q2", "a1", "y0", "m0", "B2", "A3", "W0", "a2", "y1",
+    "m1", "z0", "B3", "a3", "y2", "m2", "z1", "y3", "m3", "g0",
+    "z2", "g1", "h0", "z3", "h1", "w0", "p0", "g2", "p1", "g3",
+    "h2", "f0", "h3", "p2", "f1", "p3", "f2", "f3",
+)
 F32 = jnp.float32
 BF16 = jnp.bfloat16
 MESH = pl.DeviceIdType.MESH
@@ -98,12 +107,10 @@
     def matmul(k):
         wd_copy(k).wait()
 
-        def body(j, c):
-            cols = pl.ds(pl.multiple_of(j * W, W), W)
-            part[k, j] = jnp.dot(hid[...], wd[k, :, cols], preferred_element_type=F32).astype(BF16)
-            return c
-
-        lax.fori_loop(0, 8, body, 0)
+        for half in range(2):
+            v = jnp.dot(hid[...], wd[k, :, half * 1024:half * 1024 + 1024], preferred_element_type=F32)
+            for j in range(4):
+                part[k, half * 4 + j] = v[:, j * W:(j + 1) * W].astype(BF16)
 
     def tok(c):
         return pl.ds(CHUNKS[c][0], CHUNKS[c][1])
@@ -170,9 +177,49 @@
         lax.fori_loop(0, 4, body_b, 0)
         y3(c)[1].start()
 
+    inner = (l == 1) | (l == 2)
+    outer = (l == 0) | (l == 3)
+    low = l < 2
+    mate = quad_l(1)
+    far_in = jnp.where(low, 2, 1)
+    far_out = jnp.where(low, 3, 0)
+    at_mate = at_quad(1)
+    at_far_in = {"tensor": y * 8 + h * 4 + far_in}
+    at_far_out = {"tensor": y * 8 + h * 4 + far_out}
+    own_slot = jnp.where(l == 2, 2, 0)
+
+    def slot_of(piece):
+        return jnp.where(low, piece - 1, piece)
+
     def z1(c, m):
         dst = quad_l(m)
-        return remote(s.at[:, dst, tok(c)], zr.at[m - 1, :, tok(c)], z1s.at[m - 1, c], z1r.at[m - 1, c], at_quad(m))
+        return remote(s.at[:, dst, tok(c)], zr.at[:, m - 1, tok(c)], z1s.at[m - 1, c], z1r.at[m - 1, c], at_quad(m))
+
+    def z1_outer(c):
+        src = s.at[:, pl.ds(jnp.where(l == 0, 1, 0), 3), tok(c)]
+        return remote(src, zr.at[:, pl.ds(0, 3), tok(c)], z1s.at[0, c], z1r.at[0, c], at_mate)
+
+    def z1_inner(c):
+        return remote(s.at[:, mate, tok(c)], zr.at[:, 0, tok(c)], z1s.at[0, c], z1r.at[0, c], at_mate)
+
+    def z1_merged(c):
+        return (
+            remote(s.at[:, far_out, tok(c)], zr.at[:, 3, tok(c)], z1s.at[1, c], z1r.at[1, c], at_far_out),
+            remote(s.at[:, far_in, tok(c)], zr.at[:, 3, tok(c)], z1s.at[2, c], z1r.at[1, c], at_far_in),
+        )
+
+    def merge(c):
+        if not GATE_Z[c]:
+            return
+
+        @pl.when(inner)
+        def _():
+            z1_outer(c).wait_recv()
+            for piece, copy in zip((far_out, far_in), z1_merged(c)):
+                for hh in range(2):
+                    v = s[hh, piece, tok(c)].astype(F32) + zr[hh, slot_of(piece), tok(c)].astype(F32)
+                    s[hh, piece, tok(c)] = v.astype(BF16)
+                copy.start()
 
     def ysum(c):
         for d in y2(c) + y3(c):
@@ -184,19 +231,33 @@
             return x
 
         lax.fori_loop(0, 8, body, 0)
-        for m in (3, 2, 1):
-            z1(c, m).start()
+        if GATE_Z[c]:
+            pl.when(outer)(lambda: z1_outer(c).start())
+            pl.when(inner)(lambda: z1_inner(c).start())
+        else:
+            for m in (3, 2, 1):
+                z1(c, m).start()
 
     def z2(c):
         return remote(aggs.at[:, tok(c)], zx.at[:, tok(c)], z2s.at[c], z2r.at[c], at_half)
 
     def zsum(c):
-        for m in (1, 2, 3):
-            z1(c, m).wait_recv()
+        if c == 0:
+            c_res.wait()
+        if GATE_Z[c]:
+            pl.when(outer)(lambda: z1_inner(c).wait_recv())
+            z1_merged(c)[0].wait_recv()
+        else:
+            for m in (1, 2, 3):
+                z1(c, m).wait_recv()
 
         def body(hh, x):
-            v = s[hh, l, tok(c)].astype(F32) + zr[0, hh, tok(c)].astype(F32)
-            v = v + zr[1, hh, tok(c)].astype(F32) + zr[2, hh, tok(c)].astype(F32)
+            v = s[hh, l, tok(c)].astype(F32)
+            if GATE_Z[c]:
+                v = v + zr[hh, own_slot, tok(c)].astype(F32) + zr[hh, 3, tok(c)].astype(F32)
+            else:
+                for m in range(3):
+                    v = v + zr[hh, m, tok(c)].astype(F32)
             mine = jnp.where(hh == h, 1.0, 0.0).astype(F32)
             v = v + res[tok(c)].astype(F32) * mine
             agg[hh, tok(c)] = v
@@ -206,13 +267,30 @@
         lax.fori_loop(0, 2, body, 0)
         z2(c).start()
 
-    def g(c, m):
-        blk = sg.at[:, l, tok(c)]
-        return remote(blk, blk, gs.at[m - 1, c], gr.at[m - 1, c], at_quad(m))
-
-    def g_recv(c, m):
-        blk = sg.at[:, quad_l(m), tok(c)]
-        return remote(blk, blk, gs.at[m - 1, c], gr.at[m - 1, c], at_quad(m))
+    def g(c, i, piece, dev):
+        blk = sg.at[:, piece, tok(c)]
+        return remote(blk, blk, gs.at[i, c], gr.at[piece, c], dev)
+
+    def g_own(c):
+        if GATE_G[c]:
+            return (g(c, 0, l, at_far_in), g(c, 1, l, at_mate))
+        return tuple(g(c, m - 1, l, at_quad(m)) for m in (3, 2, 1))
+
+    def g_pass(c):
+        return (g(c, 2, far_in, at_mate), g(c, 3, far_out, at_mate))
+
+    def g_in(c, piece):
+        return g(c, 0, piece, at_mate)
+
+    def hand_on(c):
+        if not GATE_G[c]:
+            return
+
+        @pl.when(inner)
+        def _():
+            for piece, copy in zip((far_in, far_out), g_pass(c)):
+                g_in(c, piece).wait_recv()
+                copy.start()
 
     def gather(c):
         z2(c).wait_recv()
@@ -223,8 +301,7 @@
             return x
 
         lax.fori_loop(0, 2, body, 0)
-        for m in (3, 2, 1):
-            g(c, m).start()
+        start(g_own(c))
         stream_ref[tok(c)] = sg[h, l, tok(c)]
 
     def f(c, k):
@@ -235,8 +312,17 @@
 
     def project(c):
         n = CHUNKS[c][1]
-        for m in (1, 2, 3):
-            g_recv(c, m).wait_recv()
+        if GATE_G[c]:
+            g_in(c, mate).wait_recv()
+
+            @pl.when(outer)
+            def _():
+                for piece in (far_in, far_out):
+                    g_in(c, piece).wait_recv()
+        else:
+            for m in (1, 2, 3):
+                g_in(c, quad_l(m)).wait_recv()
+
         acc[:, tok(c)] = jnp.zeros((4, n, W), F32)
 
         def body(j, sq):
@@ -268,58 +354,39 @@
         extra = jnp.where((lane == NQ) | (lane == NQ + 1), v, 0.0)
         sq = jnp.sum(extra, axis=1, keepdims=True)
         v = v / jnp.sqrt(sq * (1.0 / D) + EPS)
-        qkv_ref[tok(c)] = v[:, :NQ].astype(BF16)
+        qkv_ref[tok(c)] = v
+
+    def weights_out(k):
+        q1(k).start()
+
+    def weights_on(c):
+        for k in (1, 2, 3):
+            q1_recv(k).wait_recv()
+        for m in (4, 2, 3, 5, 6, 7, 1):
+            q2(m).start()
+
+    def weights_in(c):
+        c_wq.wait()
+        c_gain.wait()
+        for m in range(1, 8):
+            q2_recv(m).wait_recv()
+
+    def first(c):
+        start(y1(c))
+
+    def plain(c):
+        start(y2(c))
 
     c_hid.wait()
     matmul(2)
     pl.semaphore_wait(barrier, len(peers))
-    start(y1(0))
-    for k in (2, 1, 3):
-        q1(k).start()
-    matmul(1)
-    y2(0)[0].start()
-    matmul(3)
-    y2(0)[1].start()
-    if NC > 1:
-        start(y1(1))
-    matmul(0)
-    c_wq.wait()
-    c_res.wait()
-    c_gain.wait()
-
-    def y_step(c):
-        aug(c)
-        if c == 0:
-            for k in (1, 2, 3):
-                q1_recv(k).wait_recv()
-            for m in (4, 2, 3, 5, 6, 7, 1):
-                q2(m).start()
-        if c + 1 < NC:
-            start(y2(c + 1))
-        if c + 2 < NC:
-            start(y1(c + 2))
-        ysum(c)
-
-    def run(stage, c):
-        if stage == 0:
-            y_step(c)
-        elif stage == 1:
-            zsum(c)
-        elif stage == 2:
-            gather(c)
-        elif stage == 3:
-            if c == 0:
-                for m in range(1, 8):
-                    q2_recv(m).wait_recv()
-            project(c)
-        else:
-            finish(c)
-
-    offsets = (0.0, 9.0, 16.0, 25.0, 30.0)
-    period = 24.0 / NC
-    order = sorted((c * period + offsets[st], st, c) for c in range(NC) for st in range(5))
-    for _, st, c in order:
-        run(st, c)
+    steps = {
+        "A": first, "B": plain, "M": matmul, "Q": weights_out, "W": weights_on, "w": weights_in,
+        "a": aug, "y": ysum, "z": zsum, "g": gather, "p": project, "f": finish,
+        "m": merge, "h": hand_on,
+    }
+    for step in ORDER:
+        steps[step[0]](int(step[1]))
 
     for k in (1, 2, 3):
         q1(k).wait_send()
@@ -328,20 +395,47 @@
     for c in range(NC):
         for d in y1(c) + y2(c) + y3(c):
             d.wait_send()
+        if GATE_Z[c]:
+            pl.when(outer)(lambda: z1_outer(c).wait_send())
+
+            @pl.when(inner)
+            def _():
+                z1_inner(c).wait_send()
+                for d in z1_merged(c):
+                    d.wait_send()
+        else:
+            for m in (1, 2, 3):
+                z1(c, m).wait_send()
+        for d in g_own(c):
+            d.wait_send()
+        if GATE_G[c]:
+
+            @pl.when(inner)
+            def _():
+                for d in g_pass(c):
+                    d.wait_send()
         for m in (1, 2, 3):
-            z1(c, m).wait_send()
-            g(c, m).wait_send()
             f(c, m).wait_send()
         z2(c).wait_send()
+
+
+def place(stream_in, qkv_in, stream_out, qkv_out, turned, sem):
+    a = pltpu.make_async_copy(stream_in, stream_out, sem.at[0])
+    a.start()
+    turned[...] = jnp.transpose(qkv_in[...])[:NQ].astype(BF16)
+    b = pltpu.make_async_copy(turned, qkv_out, sem.at[1])
+    b.start()
+    a.wait()
+    b.wait()
 
 
 def shards(hidden, down_weight, residual, norm_gain, qkv_weight):
     hbm = pl.BlockSpec(memory_space=pltpu.MemorySpace.HBM)
     vmem = pl.BlockSpec(memory_space=pltpu.VMEM)
     dma = pltpu.SemaphoreType.DMA
-    return pl.pallas_call(
+    stream, qkv = pl.pallas_call(
         kernel,
-        out_shape=(jax.ShapeDtypeStruct((T, W), BF16), jax.ShapeDtypeStruct((T, NQ), BF16)),
+        out_shape=(jax.ShapeDtypeStruct((T, W), BF16), jax.ShapeDtypeStruct((T, W), F32)),
         in_specs=[hbm] * 5,
         out_specs=(vmem, vmem),
         scratch_shapes=[
@@ -357,7 +451,7 @@
             pltpu.VMEM((8, T, W), BF16),
             pltpu.VMEM((8, T, W), BF16),
             pltpu.VMEM((2, 4, T, W), BF16),
-            pltpu.VMEM((3, 2, T, W), BF16),
+            pltpu.VMEM((2, 4, T, W), BF16),
             pltpu.VMEM((2, T, W), F32),
             pltpu.VMEM((2, T, W), BF16),
             pltpu.VMEM((2, T, W), BF16),
@@ -368,7 +462,7 @@
             dma((4,)), dma((4,)),
             dma((2, NC)), dma((2, NC)), dma((2, NC)), dma((2, NC)), dma((2, NC)), dma((2, NC)),
             dma((3, NC)), dma((3, NC)), dma((NC,)), dma((NC,)),
-            dma((3, NC)), dma((3, NC)), dma((3, NC)), dma((3, NC)),
+            dma((4, NC)), dma((4, NC)), dma((3, NC)), dma((3, NC)),
             dma((3,)), dma((3,)), dma((7,)), dma((7,)),
         ],
         compiler_params=pltpu.CompilerParams(
@@ -383,6 +477,15 @@
         norm_gain.reshape(1, D),
         qkv_weight.T,
     )
+    stream, qkv_t = pl.pallas_call(
+        place,
+        out_shape=(jax.ShapeDtypeStruct((T, W), BF16), jax.ShapeDtypeStruct((NQ, T), BF16)),
+        in_specs=[vmem, vmem],
+        out_specs=(hbm, hbm),
+        scratch_shapes=[pltpu.VMEM((NQ, T), BF16), dma((2,))],
+        name="place",
+    )(stream, qkv)
+    return (stream, qkv_t.T)
 
 
 def solution(mesh):

time: 94.1 us -> 82.4 us (0.88)
  the two profiles are of different devices: /device:TPU:256 before, /device:TPU:264 now
where the time goes in v2:
time: 82.4 us; the launch traced here: 82.2 us
  Pallas kernels  81.6 us (99%)
    pallas_call x1, Pallas kernels, shards(): pl.pallas_call(kernel, out_shape=(jax.ShapeDtypeStruct((T, W), BF16), jax...  79.8 us
    pallas_call x1, Pallas kernels, shards(): pl.pallas_call(place, out_shape=(jax.ShapeDtypeStruct((T, W), BF16), jax....  1.76 us

profile of v2, /device:TPU:264, one launch (start us, length us, event | category | flops | bytes accessed | tf_op | source)
XLA Modules:
  0.0 82.2 jit_solution(4751288344972071264)
XLA Ops:
  0.6 79.8 %down_norm_qkv.1 = (bf16[192,256]{1,0:T(8,128)(2,1)}, f32[192,256]{1,0:T(8,128)}) custom-call(bf16[192,448]{1,0:T(8,128)(2,1)} %hid_hbm.1, bf16[448,8192]{1,0:T(8,128)(2,1)} %wd_hbm.1, bf16[192,256]{1,0:T(8,128)(2,1)} %res_hbm.1, f32[1,8192]{1,0:T(1,128)} %bitcast.4, bf16[160,8192]{1,0:T(8,128)(2,1)} %bitcast.3), custom_call_target="tpu_custom_call" | custom-call | flops 1900000000 | bytes 12000000 | tf_op jit(solution)/shard_map/down_norm_qkv/pallas_call | solution.py:436
  80.4 1.8 %place.1 = (bf16[192,256]{1,0:T(8,128)(2,1)}, bf16[160,192]{1,0:T(8,128)(2,1)}) custom-call(bf16[192,256]{1,0:T(8,128)(2,1)} %get-tuple-element.6.stream_in, f32[192,256]{1,0:T(8,128)} %get-tuple-element.7.qkv_in), custom_call_target="tpu_custom_call" | custom-call | tf_op jit(solution)/shard_map/place/pallas_call | solution.py:480
